TPU v7x, 256 devices: a whole 4x4x8 slice. The times are simulated.
256 devices in a mesh: wide: 16 (over z, core), narrow: 16 (over x, y).
Axes of the slice: x: 4, y: 4, z: 8, core: 2. Of those that a mesh axis runs over, the one named last changes fastest.
Arguments:
- amplitudes: float32 [4, 64, 640, 640], P(None, 'wide', None, 'narrow'), may hold values from -6 to 6
- cycle_block: float32 [64, 640, 4, 640], P('wide', 'narrow'), may hold values from -0.078125 to 0.078125
- occupied_irreps: int32 [64], replicated, may hold values from 0 to 7, as said below
- virtual_irreps: int32 [640], replicated, may hold values from 0 to 7, as said below
- slab_orbitals: int32 [4], replicated, may hold values from 0 to 63, as said below
Outputs:
- cycle_residual: float32 [4, 4, 640, 640], P(None, None, 'narrow', 'wide')
Inputs may be any that keep to these rules, and one draw needn't show every extreme that they name: `occupied_irreps`: nondecreasing; every irrep 0 to 7 labels at least 4 orbitals. `virtual_irreps`: nondecreasing; every irrep 0 to 7 labels at least 64 orbitals. `slab_orbitals`: distinct occupied orbital indices in increasing order; the last is 63.
All inputs are finite; a program needn't handle non-finite values.
Results may differ from a plain program's by a relative error of at most 0.0003.
Values sent between devices are 32-bit elements; how exact they have to be, the bound alone decides.
No kernel may reach another device: no remote copies, remote signals or barrier semaphores. Data moves between devices by JAX's collectives and lax.ppermute only.
A program may use at most 128 MiB of HBM per device.

v0:
```python
import functools

import jax
import jax.numpy as jnp
import numpy as np
from jax import lax
from jax.experimental import pallas as pl
from jax.experimental.pallas import tpu as pltpu
from jax.sharding import PartitionSpec as P

SMEM = pl.BlockSpec(memory_space=pltpu.SMEM)
VMEM = pl.BlockSpec(memory_space=pltpu.VMEM)
LIMIT = 48 * 1024 * 1024
CLASSES = 8
PACKED, ANY = 192, 512
SHORT, ALL = 6, 16
SLAB, FORM, PLACE, COUNT, SHIFT = 8, 12, 16, 32, 64


def params():
    return pltpu.CompilerParams(vmem_limit_bytes=LIMIT)


def iota(shape, dim):
    return lax.broadcasted_iota(jnp.int32, shape, dim)


def class_of(table, index):
    label = jnp.zeros_like(index)
    for x in range(1, CLASSES):
        label = label + (index >= table[x]).astype(jnp.int32)
    return label


def table_kernel(occ, vir, slab, table):
    v = vir[...].astype(jnp.float32)
    table[0] = 0
    starts = [jnp.int32(0)]
    for x in range(1, CLASSES):
        start = jnp.sum((v < x).astype(jnp.float32)).astype(jnp.int32)
        table[x] = start
        starts.append(start)
    starts.append(jnp.int32(vir.shape[0] * vir.shape[1]))

    def before(t, half):
        rest = lax.rem(t, 80) - 40 * half
        return lax.div(t, 80) * 40 + jnp.minimum(jnp.maximum(rest, 0), 40)

    marks = [[before(t, half) for t in starts] for half in range(2)]
    for half in range(2):
        for x in range(CLASSES):
            table[COUNT + 8 * half + x] = marks[half][x + 1] - marks[half][x]
    s = [occ[slab[i]] for i in range(4)]
    for i in range(4):
        table[SLAB + i] = s[i]
    labels = [s[i] ^ s[j] for i in range(4) for j in range(4)]
    most = jnp.int32(0)
    for p in range(16):
        place = jnp.int32(0)
        for r in range(p):
            place = place + (labels[r] == labels[p]).astype(jnp.int32)
        table[PLACE + p] = place
        most = jnp.maximum(most, place)
    widest = jnp.int32(0)
    for half in range(2):
        for j in range(4):
            for x in range(CLASSES):
                offset = jnp.int32(0)
                for other in range(j):
                    offset = offset + table[COUNT + 8 * half + (x ^ s[j] ^ s[other])]
                table[SHIFT + 32 * half + 8 * j + x] = offset - marks[half][x]
                if j == 3:
                    widest = jnp.maximum(widest, offset + table[COUNT + 8 * half + x])
    packed = (widest <= PACKED).astype(jnp.int32)
    table[FORM] = packed * (1 + (most < SHORT).astype(jnp.int32))


def make_table(occ, vir, slab):
    return pl.pallas_call(
        table_kernel,
        out_shape=jax.ShapeDtypeStruct((128,), jnp.int32),
        in_specs=[SMEM, VMEM, SMEM],
        out_specs=SMEM,
        name="table",
    )(occ, vir.reshape(5, 128), slab)


def row_labels(table, occ, wide, narrow):
    row = iota((160, 1), 0)
    k = (row >= 40).astype(jnp.int32) + (row >= 80).astype(jnp.int32) + (row >= 120).astype(jnp.int32)
    label = jnp.zeros_like(row)
    for q in range(4):
        label = jnp.where(k == q, occ[wide * 4 + q], label)
    return label ^ class_of(table, row - 40 * k + 40 * narrow)


def halves(x):
    hi = x.astype(jnp.bfloat16)
    return hi, (x - hi.astype(jnp.float32)).astype(jnp.bfloat16)


def fold_kernel(lanes, table, occ, w, own, other):
    wide, narrow = lax.axis_index("wide"), lax.axis_index("narrow")
    rows = row_labels(table, occ, wide, narrow)
    b = iota((1, 640), 1)
    cols = class_of(table, b)
    block = jnp.zeros_like(b)
    for t in range(1, 16):
        block = block + (b >= 40 * t).astype(jnp.int32)
    half = block & 1
    u = b - 40 * (block - (block >> 1))
    column = iota((lanes, 640), 0)
    mine = lax.rem(wide, 2)
    sums = [None, None]
    for j in range(4):
        keep = (rows ^ table[SLAB + j]) == cols
        hi, lo = halves(jnp.where(keep, w[:, j, :], 0.0))
        for side, at in enumerate((mine, 1 - mine)):
            shift = jnp.zeros_like(b)
            for x in range(CLASSES):
                shift = jnp.where(cols == x, table[SHIFT + 32 * at + 8 * j + x], shift)
            pick = (column == jnp.where(half == at, u + shift, -1)).astype(jnp.float32).astype(jnp.bfloat16)
            for part in (hi, lo):
                term = lax.dot_general(part, pick, (((1,), (1,)), ((), ())), preferred_element_type=jnp.float32)
                sums[side] = term if sums[side] is None else sums[side] + term
    own[...] = sums[0]
    other[...] = sums[1]


def fold(lanes, table, occ, w):
    shape = jax.ShapeDtypeStruct((160, lanes), jnp.float32)
    own, other = pl.pallas_call(
        functools.partial(fold_kernel, lanes),
        out_shape=(shape, shape),
        in_specs=[SMEM, SMEM, VMEM],
        out_specs=(VMEM, VMEM),
        compiler_params=params(),
        name="fold",
    )(table, occ, w)
    return own, swap(other)


def swap(x):
    return lax.ppermute(x, "wide", [(d, d ^ 1) for d in range(16)])


def product_kernel(lanes, table, occ, a_own, a_other, w_own, w_other, out):
    wide, narrow = lax.axis_index("wide"), lax.axis_index("narrow")
    w0, v0 = halves(w_own[...])
    w1, v1 = halves(w_other[...])
    right = jnp.concatenate([w0, w1, w0, w1, v0, v1], axis=0)
    rows = [row_labels(table, occ, at, narrow) for at in (wide, wide ^ 1)]
    both = []
    for step in range(2):
        cols = class_of(table, iota((1, 640), 1)) ^ table[SLAB + 2 * pl.program_id(0) + step]
        his, los = [], []
        for a, row in zip((a_own, a_other), rows):
            hi, lo = halves(jnp.where(row == cols, a[step], 0.0))
            his.append(hi)
            los.append(lo)
        left = jnp.concatenate(his + los + his, axis=0)
        r = lax.dot_general(left, right, (((0,), (0,)), ((), ())), preferred_element_type=jnp.float32)
        if lanes == 256:
            out[:, 40 * step:40 * step + 40, :] = r[:, :128].reshape(16, 40, 128)
            both.append(r[:, 128:])
        else:
            out[:, 40 * step:40 * step + 40, :] = r.reshape(16, 40, lanes)
    if both:
        tails = jnp.where(iota((640, 128), 1) < 64, both[0], pltpu.roll(both[1], 64, 1))
        out[:, 80:, :] = tails.reshape(16, 40, 128)


def product(lanes, table, occ, a_own, a_other, w_own, w_other):
    block = pl.BlockSpec((2, 160, 640), lambda p: (p, 0, 0))
    whole = pl.BlockSpec((160, lanes), lambda p: (0, 0))
    rows, wide = (120, 128) if lanes == 256 else (80, lanes)
    return pl.pallas_call(
        functools.partial(product_kernel, lanes),
        out_shape=jax.ShapeDtypeStruct((16, 2 * rows, wide), jnp.float32),
        grid=(2,),
        in_specs=[SMEM, SMEM, block, block, whole, whole],
        out_specs=pl.BlockSpec((16, rows, wide), lambda p: (0, p, 0)),
        compiler_params=params(),
        name="product",
    )(table, occ, a_own, a_other, w_own, w_other)


def spread_kernel(lanes, q, table, got, out, acc):
    wide, narrow = lax.axis_index("wide"), lax.axis_index("narrow")
    core = lax.rem(wide, 2)
    acls = class_of(table, iota((40, 1), 0) + 40 * narrow)
    u = iota((1, 384), 1)
    block = jnp.zeros_like(u)
    for t in range(1, 8):
        block = block + (u >= 40 * t).astype(jnp.int32)
    bcls = class_of(table, u + 40 * block + 40 * core)
    first, last = jnp.int32(0), jnp.int32(0)
    for x in range(1, CLASSES):
        first = first + (40 * narrow >= table[x]).astype(jnp.int32)
        last = last + (40 * narrow + 39 >= table[x]).astype(jnp.int32)
    acc[...] = jnp.zeros_like(acc)
    span = 80 if lanes == 512 else 120
    for p in range(2):
        r = got[0, p * span:(p + 1) * span, :]
        for n in range(1, 16):
            r = r + got[n, p * span:(p + 1) * span, :]
        for step in range(2):
            i = 2 * p + step
            value = r[40 * step:40 * step + 40]
            if lanes == 256:
                tail = r[80:] if step == 0 else pltpu.roll(r[80:], 64, 1)
                value = jnp.concatenate([value, tail, tail], axis=1)
            size = value.shape[1]
            for j in range(4):
                pair = table[SLAB + i] ^ table[SLAB + j]
                at = table[PLACE + 4 * i + j]
                x, y = first ^ pair, last ^ pair
                shift = table[SHIFT + 32 * core + 8 * j + x]
                one = pltpu.roll(value, lax.rem(size - shift, size), 1)[:, :384]
                shift = table[SHIFT + 32 * core + 8 * j + y]
                two = pltpu.roll(value, lax.rem(size - shift, size), 1)[:, :384]
                found = jnp.where(acls == first, one, two)
                acc[at] += jnp.where((acls ^ bcls) == pair, found, 0.0)
    pad = out.shape[2] - 40 * q
    for z in range(8):
        pieces = [acc[p, :, 40 * z:40 * z + 40] for p in range(q)]
        if pad:
            pieces.append(jnp.zeros((40, pad), jnp.float32))
        out[z] = jnp.concatenate(pieces, axis=1)


def spread(lanes, q, table, got):
    wide = -(-40 * q // 128) * 128
    return pl.pallas_call(
        functools.partial(spread_kernel, lanes, q),
        out_shape=jax.ShapeDtypeStruct((8, 40, wide), jnp.float32),
        in_specs=[SMEM, VMEM],
        out_specs=VMEM,
        scratch_shapes=[pltpu.VMEM((q, 40, 384), jnp.float32)],
        compiler_params=params(),
        name="spread",
    )(table, got)


def finish_kernel(q, table, got, out, acc):
    wide, narrow = lax.axis_index("wide"), lax.axis_index("narrow")
    acls = class_of(table, iota((40, 1), 0) + 40 * narrow)
    plane = acls ^ class_of(table, iota((1, 40), 1) + 40 * wide)
    r = got[0]
    for z in range(1, 8):
        r = r + got[z]
    for p in range(q):
        acc[p] = r[:, 40 * p:40 * p + 40]
    for i in range(4):
        for j in range(4):
            keep = plane == (table[SLAB + i] ^ table[SLAB + j])
            out[i, j] = jnp.where(keep, acc[table[PLACE + 4 * i + j]], 0.0)


def finish(q, table, got):
    return pl.pallas_call(
        functools.partial(finish_kernel, q),
        out_shape=jax.ShapeDtypeStruct((4, 4, 40, 40), jnp.float32),
        in_specs=[SMEM, VMEM],
        out_specs=VMEM,
        scratch_shapes=[pltpu.VMEM((q, 40, 40), jnp.float32)],
        compiler_params=params(),
        name="finish",
    )(table, got)


def rest(lanes, q, table, occ, a_own, a_other, w_own, w_other):
    sent = product(lanes, table, occ, a_own, a_other, w_own, w_other)
    got = lax.all_to_all(sent, "narrow", 0, 0)
    slots = spread(lanes, q, table, got)
    same_core = [[c + 2 * z for z in range(8)] for c in range(2)]
    return finish(q, table, lax.all_to_all(slots, "wide", 0, 0, axis_index_groups=same_core))


def local(amplitudes, cycle_block, occ, vir, slab):
    a_own = jnp.transpose(amplitudes, (0, 1, 3, 2)).reshape(4, 160, 640)
    a_other = swap(a_own)
    w = cycle_block.reshape(160, 4, 640)
    table = make_table(occ, vir, slab)
    w_own, w_other = fold(256, table, occ, w)

    def general(w, w_own, w_other):
        own, other = fold(ANY, table, occ, w)
        return rest(ANY, ALL, table, occ, a_own, a_other, own, other)

    def packed(w, w_own, w_other):
        return rest(256, ALL, table, occ, a_own, a_other, w_own, w_other)

    def short(w, w_own, w_other):
        return rest(256, SHORT, table, occ, a_own, a_other, w_own, w_other)

    return lax.switch(table[FORM], [general, packed, short], w, w_own, w_other)


def solution(mesh):
    placed = (P(None, "wide", None, "narrow"), P("wide", "narrow", None, None), P(), P(), P())
    return jax.shard_map(
        local,
        mesh=mesh,
        in_specs=placed,
        out_specs=P(None, None, "narrow", "wide"),
        check_vma=False,
    )
```

profile of v0, /device:TPU:2, one launch (start us, length us, event | category | flops | bytes accessed | tf_op | source)
XLA Modules:
  0.0 67.1 jit_solution(2423130279833331558)
XLA Ops:
  0.0 0.0 collective-permute-start.1
  0.0 1.9 %table.1 = s32[128]{0:T(128)S(1)} custom-call(s32[64]{0:T(128)} %occ.3, s32[5,128]{1,0:T(8,128)} %bitcast.12, s32[4]{0:T(128)} %slab.1), custom_call_target="tpu_custom_call" | custom-call | tf_op jit(solution)/shard_map/table/pallas_call | solution.py:79
  1.9 4.0 %fold.3 = (f32[160,256]{1,0:T(8,128)S(1)}, f32[160,256]{1,0:T(8,128)S(1)}) custom-call(s32[128]{0:T(128)S(1)} %table.1, s32[64]{0:T(128)} %occ.3, f32[160,4,640]{2,1,0:T(4,128)} %bitcast.10), custom_call_target="tpu_custom_call" | custom-call | tf_op jit(solution)/shard_map/fold/pallas_call | solution.py:132
  5.9 0.6 collective-permute-start.2
  6.5 0.6 slice.3
  7.7 0.0 collective-permute-done.1
  7.7 0.0 collective-permute-done.2
  7.7 58.6 %conditional.1 = (f32[4,4,40,40]{3,2,1,0:T(8,128)S(1)}) conditional(s32[]{:T(128)} %bitcast.1, (s32[128]{0:T(128)S(1)}, s32[64]{0:T(128)}, f32[160,4,640]{2,1,0:T(4,128)}, f32[4,160,640]{2,1,0:T(8,128)}, f32[4,160,640]{2,1,0:T(8,128)S(1)}) %tuple.25, (s32[128]{0:T(128)S(1)}, s32[64]{0:T(128)}, f32[4,160,640]{2,1,0:T(8,128)}, ...), branch_computations={%region_0.0_spmd, %region_1.0_spmd, %region_2.0_spmd} | conditional | bytes 19988556 | solution.py:297
  8.0 3.3 %product.5 = f32[16,240,128]{2,1,0:T(8,128)S(1)} custom-call(s32[128]{0:T(128)S(1)} %get-tuple-element.56.table, s32[64]{0:T(128)} %get-tuple-element.57.occ, f32[4,160,640]{2,1,0:T(8,128)} %get-tuple-element.58.a_own, f32[4,160,640]{2,1,0:T(8,128)S(1)} %get-tuple-element.59.a_other, f32[160,256]{1,0:T(8,128)S(1)} %get-tuple-element.60.w_own, ...), custom_call_target="tpu_custom_call" | custom-call | tf_op jit(solution)/shard_map/cond/branch_2_fun/product/pallas_call | solution.py:177
  11.3 32.5 %all_to_all.28.got = f32[16,240,128]{2,1,0:T(8,128)S(1)} all-to-all(f32[16,240,128]{2,1,0:T(8,128)S(1)} %product.5), channel_id=1, replica_groups=mesh['wide'=16,'narrow'=16] {'narrow'}, dimensions={0} | all-to-all | bytes 3932160 | tf_op jit(solution)/shard_map/cond/branch_2_fun/all_to_all | solution.py:274
  43.8 1.5 %spread.5 = f32[8,40,256]{2,1,0:T(8,128)S(1)} custom-call(s32[128]{0:T(128)S(1)} %get-tuple-element.56.table, f32[16,240,128]{2,1,0:T(8,128)S(1)} %all_to_all.28.got), custom_call_target="tpu_custom_call" | custom-call | tf_op jit(solution)/shard_map/cond/branch_2_fun/spread/pallas_call | solution.py:234
  45.3 20.1 %all_to_all.29.got = f32[8,40,256]{2,1,0:T(8,128)S(1)} all-to-all(f32[8,40,256]{2,1,0:T(8,128)S(1)} %spread.5), channel_id=1, replica_groups={{0,32,64,96,128,160,192,224},{16,48,80,112,144,176,208,240},{1,33,65,97..., dimensions={0} | all-to-all | bytes 655360 | tf_op jit(solution)/shard_map/cond/branch_2_fun/all_to_all | solution.py:277
  65.4 0.7 finish.5
  66.3 0.0 copy-start.1
  66.4 0.7 %copy-done.1 = f32[4,4,40,40]{3,2,1,0:T(8,128)} copy-done((f32[4,4,40,40]{3,2,1,0:T(8,128)}, f32[4,4,40,40]{3,2,1,0:T(8,128)S(1)}, u32[]{:S(2)}) %copy-start.1) | copy-done | bytes 102424
Async XLA Ops:
  0.0 7.7 %collective-permute-start.1 = (f32[4,160,640]{2,1,0:T(8,128)}, f32[4,160,640]{2,1,0:T(8,128)S(1)}, u32[]{:S(2)}, u32[]{:S(2)}) collective-permute-start(f32[4,160,640]{2,1,0:T(8,128)} %bitcast.6), channel_id=1, source_target_pairs={{0,16},{16,0},{32,48},{48,32},{64,80},{80,64},{96,112},{112,96},{1... | collective-permute-start | bytes 4915208 | tf_op jit(solution)/shard_map/ppermute | solution.py:144
  5.9 1.8 %collective-permute-start.2 = (f32[160,256]{1,0:T(8,128)S(1)}, f32[160,256]{1,0:T(8,128)S(1)}, u32[]{:S(2)}, u32[]{:S(2)}) collective-permute-start(f32[160,256]{1,0:T(8,128)S(1)} %get-tuple-element.65), channel_id=1, source_target_pairs={{0,16},{16,0},{32,48},{48,32},{64,80},{80,64},{96,112},{112,96},{1... | collective-permute-start | bytes 491528 | tf_op jit(solution)/shard_map/ppermute | solution.py:144
  66.3 0.7 %copy-start.1 = (f32[4,4,40,40]{3,2,1,0:T(8,128)}, f32[4,4,40,40]{3,2,1,0:T(8,128)S(1)}, u32[]{:S(2)}) copy-start(f32[4,4,40,40]{3,2,1,0:T(8,128)S(1)} %get-tuple-element.76) | copy-start | bytes 307204
where the time goes:
time: 67.3 us; the launch traced here: 67.1 us
  blocking collectives  52.6 us (78%)
  Pallas kernels  11.3 us (17%)
  local copies, waits for them, and re-layouts  1.3 us (2%)
  between operations  0.7 us (1%)
    all_to_all x1, blocking collectives, rest(): got = lax.all_to_all(sent, 'narrow', 0, 0)  32.5 us
    all_to_all x1, blocking collectives, rest(): lax.all_to_all(slots, 'wide', 0, 0, axis_index_groups=same_core)  20.1 us
    pallas_call x1, Pallas kernels, fold(): pl.pallas_call(functools.partial(fold_kernel, lanes), out_shape=(shape, s...  3.96 us
    pallas_call x1, Pallas kernels, product(): pl.pallas_call(functools.partial(product_kernel, lanes), out_shape=jax.Sh...  3.3 us
    pallas_call x1, Pallas kernels, make_table(): pl.pallas_call(table_kernel, out_shape=jax.ShapeDtypeStruct((128,), jnp.i...  1.9 us
    pallas_call x1, Pallas kernels, spread(): pl.pallas_call(functools.partial(spread_kernel, lanes, q), out_shape=jax....  1.49 us
  transfers between devices with their start and end apart: 2, of which 0 were waited for; matrix products, arithmetic and copies ran while one was open for 1% of the time, Pallas kernels for 9%

commit v1 on v0

v1 whole, which is shorter than its diff:
```python
import functools

import jax
import jax.numpy as jnp
import numpy as np
from jax import lax
from jax.experimental import pallas as pl
from jax.experimental.pallas import tpu as pltpu
from jax.sharding import PartitionSpec as P

SMEM = pl.BlockSpec(memory_space=pltpu.SMEM)
VMEM = pl.BlockSpec(memory_space=pltpu.VMEM)
LIMIT = 48 * 1024 * 1024
CLASSES = 8
TIGHT, PACKED, ANY = 170, 192, 512
LEAST, SHORT, ALL = 4, 6, 16
SLAB, PLACE, COUNT, SHIFT = 8, 16, 32, 64


def params():
    return pltpu.CompilerParams(vmem_limit_bytes=LIMIT)


def iota(shape, dim):
    return lax.broadcasted_iota(jnp.int32, shape, dim)


def class_of(table, index):
    label = jnp.zeros_like(index)
    for x in range(1, CLASSES):
        label = label + (index >= table[x]).astype(jnp.int32)
    return label


def fill_table(occ, vir, slab, table, form):
    v = vir[...].astype(jnp.float32)
    table[0] = 0
    starts = [jnp.int32(0)]
    for x in range(1, CLASSES):
        start = jnp.sum((v < x).astype(jnp.float32)).astype(jnp.int32)
        table[x] = start
        starts.append(start)
    starts.append(jnp.int32(vir.shape[0] * vir.shape[1]))

    def before(t, half):
        rest = lax.rem(t, 80) - 40 * half
        return lax.div(t, 80) * 40 + jnp.minimum(jnp.maximum(rest, 0), 40)

    marks = [[before(t, half) for t in starts] for half in range(2)]
    for half in range(2):
        for x in range(CLASSES):
            table[COUNT + 8 * half + x] = marks[half][x + 1] - marks[half][x]
    s = [occ[slab[i]] for i in range(4)]
    for i in range(4):
        table[SLAB + i] = s[i]
    labels = [s[i] ^ s[j] for i in range(4) for j in range(4)]
    most = jnp.int32(0)
    for p in range(16):
        place = jnp.int32(0)
        for r in range(p):
            place = place + (labels[r] == labels[p]).astype(jnp.int32)
        table[PLACE + p] = place
        most = jnp.maximum(most, place)
    widest = jnp.int32(0)
    for half in range(2):
        for j in range(4):
            for x in range(CLASSES):
                offset = jnp.int32(0)
                for other in range(j):
                    offset = offset + table[COUNT + 8 * half + (x ^ s[j] ^ s[other])]
                table[SHIFT + 32 * half + 8 * j + x] = offset - marks[half][x]
                if j == 3:
                    widest = jnp.maximum(widest, offset + table[COUNT + 8 * half + x])
    packed = (widest <= PACKED).astype(jnp.int32)
    form[0] = packed * (1 + (most < SHORT).astype(jnp.int32))


def row_labels(table, occ, wide, narrow):
    row = iota((160, 1), 0)
    k = (row >= 40).astype(jnp.int32) + (row >= 80).astype(jnp.int32) + (row >= 120).astype(jnp.int32)
    label = jnp.zeros_like(row)
    for q in range(4):
        label = jnp.where(k == q, occ[wide * 4 + q], label)
    return label ^ class_of(table, row - 40 * k + 40 * narrow)


def halves(x):
    hi = x.astype(jnp.bfloat16)
    return hi, (x - hi.astype(jnp.float32)).astype(jnp.bfloat16)


def fold_halves(lanes, table, occ, w, own, other):
    wide, narrow = lax.axis_index("wide"), lax.axis_index("narrow")
    rows = row_labels(table, occ, wide, narrow)
    b = iota((1, 640), 1)
    cols = class_of(table, b)
    block = jnp.zeros_like(b)
    for t in range(1, 16):
        block = block + (b >= 40 * t).astype(jnp.int32)
    half = block & 1
    u = b - 40 * (block - (block >> 1))
    column = iota((lanes, 640), 0)
    mine = lax.rem(wide, 2)
    left, picks = [], [[], []]
    for j in range(4):
        keep = (rows ^ table[SLAB + j]) == cols
        left.append(jnp.concatenate(halves(jnp.where(keep, w[:, j, :], 0.0)), axis=0))
        for side, at in enumerate((mine, 1 - mine)):
            shift = jnp.zeros_like(b)
            for x in range(CLASSES):
                shift = jnp.where(cols == x, table[SHIFT + 32 * at + 8 * j + x], shift)
            place = jnp.where(half == at, u + shift, -1)
            picks[side].append((column == place).astype(jnp.float32).astype(jnp.bfloat16))
    left = jnp.concatenate(left, axis=1)
    for side, out in enumerate((own, other)):
        pick = jnp.concatenate(picks[side], axis=1)
        r = lax.dot_general(left, pick, (((1,), (1,)), ((), ())), preferred_element_type=jnp.float32)
        out[:, :lanes] = r[:160] + r[160:]
        if lanes < out.shape[1]:
            out[:, lanes:] = jnp.zeros((160, out.shape[1] - lanes), jnp.float32)


def first_kernel(occ, vir, slab, w, table, form, own, other, held, sem):
    copy = pltpu.make_async_copy(w, held, sem)
    copy.start()
    fill_table(occ, vir, slab, table, form)
    copy.wait()
    fold_halves(PACKED, table, occ, held, own, other)


def first(occ, vir, slab, w):
    shape = jax.ShapeDtypeStruct((160, 256), jnp.float32)
    return pl.pallas_call(
        first_kernel,
        out_shape=(jax.ShapeDtypeStruct((128,), jnp.int32), jax.ShapeDtypeStruct((1,), jnp.int32), shape, shape),
        in_specs=[SMEM, VMEM, SMEM, pl.BlockSpec(memory_space=pltpu.HBM)],
        out_specs=(SMEM, SMEM, VMEM, VMEM),
        scratch_shapes=[pltpu.VMEM((160, 4, 640), jnp.float32), pltpu.SemaphoreType.DMA],
        compiler_params=params(),
        name="first",
    )(occ, vir.reshape(5, 128), slab, w)


def fold_any(table, occ, w):
    shape = jax.ShapeDtypeStruct((160, ANY), jnp.float32)
    return pl.pallas_call(
        functools.partial(fold_halves, ANY),
        out_shape=(shape, shape),
        in_specs=[SMEM, SMEM, VMEM],
        out_specs=(VMEM, VMEM),
        compiler_params=params(),
        name="fold",
    )(table, occ, w)


def swap(x):
    return lax.ppermute(x, "wide", [(d, d ^ 1) for d in range(16)])


def beside(parts, step):
    lane = iota(parts[0].shape, 1)
    out = parts[0]
    for t in range(1, len(parts)):
        out = jnp.where(lane < step * t, out, pltpu.roll(parts[t], step * t, 1))
    return out


def product_kernel(form, table, occ, a_own, a_other, w_own, w_other, out):
    wide, narrow = lax.axis_index("wide"), lax.axis_index("narrow")
    w0, v0 = halves(w_own[...])
    w1, v1 = halves(w_other[...])
    right = jnp.concatenate([w0, w1, w0, w1, v0, v1], axis=0)
    rows = [row_labels(table, occ, at, narrow) for at in (wide, wide ^ 1)]
    tails = []
    for i in range(4):
        cols = class_of(table, iota((1, 640), 1)) ^ table[SLAB + i]
        his, los = [], []
        for a, row in zip((a_own, a_other), rows):
            hi, lo = halves(jnp.where(row == cols, a[i], 0.0))
            his.append(hi)
            los.append(lo)
        left = jnp.concatenate(his + los + his, axis=0)
        r = lax.dot_general(left, right, (((0,), (0,)), ((), ())), preferred_element_type=jnp.float32)
        width = out.shape[2]
        out[:, 40 * i:40 * i + 40, :] = r[:, :width].reshape(16, 40, width)
        tails.append(r[:, 128:256])
    if form == PACKED:
        out[:, 160:200, :] = beside(tails[:2], 64).reshape(16, 40, 128)
        out[:, 200:240, :] = beside(tails[2:], 64).reshape(16, 40, 128)
    elif form == TIGHT:
        out[:, 160:200, :] = beside(tails[:3], 42).reshape(16, 40, 128)
        lane = iota((16, 16, 128), 2)
        last = [pltpu.roll(tails[3], 42 * t, 1) if t else tails[3] for t in range(3)]
        last = [x.reshape(16, 40, 128)[:, at:at + 16] for x, at in zip(last, (0, 16, 24))]
        out[:, 200:216, :] = jnp.where(lane < 42, last[0], jnp.where(lane < 84, last[1], last[2]))


def product(form, table, occ, a_own, a_other, w_own, w_other):
    shape = {TIGHT: (16, 216, 128), PACKED: (16, 240, 128), ANY: (16, 160, 512)}[form]
    return pl.pallas_call(
        functools.partial(product_kernel, form),
        out_shape=jax.ShapeDtypeStruct(shape, jnp.float32),
        in_specs=[SMEM, SMEM, VMEM, VMEM, VMEM, VMEM],
        out_specs=VMEM,
        compiler_params=params(),
        name="product",
    )(table, occ, a_own, a_other, w_own, w_other)


def tail_of(form, r, i):
    if form == PACKED:
        rows = r[160 + 40 * (i // 2):200 + 40 * (i // 2)]
        return pltpu.roll(rows, 64, 1) if i % 2 else rows
    if i < 3:
        return pltpu.roll(r[160:200], 128 - 42 * i, 1) if i else r[160:200]
    rows = r[200:216]
    return jnp.concatenate([rows, pltpu.roll(rows, 86, 1), pltpu.roll(rows, 44, 1)[8:16]], axis=0)


def spread_kernel(form, q, table, got, out, acc):
    wide, narrow = lax.axis_index("wide"), lax.axis_index("narrow")
    core = lax.rem(wide, 2)
    acls = class_of(table, iota((40, 1), 0) + 40 * narrow)
    u = iota((1, 384), 1)
    block = jnp.zeros_like(u)
    for t in range(1, 8):
        block = block + (u >= 40 * t).astype(jnp.int32)
    bcls = class_of(table, u + 40 * block + 40 * core)
    first, last = jnp.int32(0), jnp.int32(0)
    for x in range(1, CLASSES):
        first = first + (40 * narrow >= table[x]).astype(jnp.int32)
        last = last + (40 * narrow + 39 >= table[x]).astype(jnp.int32)
    acc[...] = jnp.zeros_like(acc)
    r = got[0]
    for n in range(1, 16):
        r = r + got[n]
    for i in range(4):
        value = r[40 * i:40 * i + 40]
        if form != ANY:
            tail = tail_of(form, r, i)
            value = jnp.concatenate([value, tail, tail], axis=1)
        size = value.shape[1]
        for j in range(4):
            pair = table[SLAB + i] ^ table[SLAB + j]
            at = table[PLACE + 4 * i + j]
            x, y = first ^ pair, last ^ pair
            shift = table[SHIFT + 32 * core + 8 * j + x]
            one = pltpu.roll(value, lax.rem(size - shift, size), 1)[:, :384]
            shift = table[SHIFT + 32 * core + 8 * j + y]
            two = pltpu.roll(value, lax.rem(size - shift, size), 1)[:, :384]
            found = jnp.where(acls == first, one, two)
            acc[at] += jnp.where((acls ^ bcls) == pair, found, 0.0)
    pad = -40 * q % 128
    for z in range(8):
        pieces = [acc[p, :, 40 * z:40 * z + 40] for p in range(q)]
        if pad:
            pieces.append(jnp.zeros((40, pad), jnp.float32))
        slot = jnp.concatenate(pieces, axis=1)
        if q == LEAST:
            out[z, :40] = slot[:, :128]
            groups = [slot[0:16, 128:160], slot[16:32, 128:160], slot[24:40, 128:160], slot[0:16, 160:192]]
            out[z, 40:] = jnp.concatenate(groups, axis=1)
        else:
            out[z] = slot


def slot_shape(q):
    return (8, 56, 128) if q == LEAST else (8, 40, -(-40 * q // 128) * 128)


def spread(form, q, table, got):
    return pl.pallas_call(
        functools.partial(spread_kernel, form, q),
        out_shape=jax.ShapeDtypeStruct(slot_shape(q), jnp.float32),
        in_specs=[SMEM, VMEM],
        out_specs=VMEM,
        scratch_shapes=[pltpu.VMEM((q, 40, 384), jnp.float32)],
        compiler_params=params(),
        name="spread",
    )(table, got)


def finish_kernel(q, table, got, out, acc):
    wide, narrow = lax.axis_index("wide"), lax.axis_index("narrow")
    acls = class_of(table, iota((40, 1), 0) + 40 * narrow)
    plane = acls ^ class_of(table, iota((1, 40), 1) + 40 * wide)
    r = got[0]
    for z in range(1, 8):
        r = r + got[z]
    if q == LEAST:
        tail = jnp.concatenate([r[40:, 0:32], r[40:, 32:64], r[48:, 64:96]], axis=0)
        r = jnp.concatenate([r[:40], tail], axis=1)
    for p in range(q):
        acc[p] = r[:, 40 * p:40 * p + 40]
    for i in range(4):
        for j in range(4):
            keep = plane == (table[SLAB + i] ^ table[SLAB + j])
            out[i, j] = jnp.where(keep, acc[table[PLACE + 4 * i + j]], 0.0)


def finish(q, table, got):
    shape = (4, 4, 40, 40)
    return pl.pallas_call(
        functools.partial(finish_kernel, q),
        out_shape=jax.ShapeDtypeStruct(shape, jnp.float32),
        in_specs=[SMEM, VMEM],
        out_specs=VMEM,
        scratch_shapes=[pltpu.VMEM((q, 40, 40), jnp.float32)],
        compiler_params=params(),
        name="finish",
    )(table, got)


def rest(form, q, table, occ, a_own, a_other, w_own, w_other):
    sent = product(form, table, occ, a_own, a_other, w_own, w_other)
    got = lax.all_to_all(sent, "narrow", 0, 0)
    slots = spread(form, q, table, got)
    same_core = [[c + 2 * z for z in range(8)] for c in range(2)]
    return finish(q, table, lax.all_to_all(slots, "wide", 0, 0, axis_index_groups=same_core))


def local(amplitudes, cycle_block, occ, vir, slab):
    a_own = jnp.transpose(amplitudes, (0, 1, 3, 2)).reshape(4, 160, 640)
    a_other = swap(a_own)
    w = cycle_block.reshape(160, 4, 640)
    table, form, w_own, w_other = first(occ, vir, slab, w)
    w_other = swap(w_other)

    def general(w, w_own, w_other):
        own, other = fold_any(table, occ, w)
        return rest(ANY, ALL, table, occ, a_own, a_other, own, swap(other))

    def packed(form, q):
        return lambda w, w_own, w_other: rest(form, q, table, occ, a_own, a_other, w_own, w_other)

    forms = [general, packed(PACKED, ALL), packed(PACKED, SHORT)]
    return lax.switch(form.reshape(()), forms, w, w_own, w_other)


def solution(mesh):
    placed = (P(None, "wide", None, "narrow"), P("wide", "narrow", None, None), P(), P(), P())
    return jax.shard_map(
        local,
        mesh=mesh,
        in_specs=placed,
        out_specs=P(None, None, "narrow", "wide"),
        check_vma=False,
    )
```

time: 67.3 us -> 67.3 us (level); the launches traced: 67.1 us -> 66.3 us
  Pallas kernels: 11.3 us -> 9.4 us
  local copies, waits for them, and re-layouts: 1.3 us -> 2.06 us
    pallas_call x4 -> x3, Pallas kernels: 10.6 us -> 8.73 us  [the longest x1 4.12 us: first(): pl.pallas_call(first_kernel, out_shape=(jax.ShapeDtypeStruct((128,), jnp....]
    unnamed x2 -> x6, local copies, waits for them, and re-layouts: 0.72 us -> 2.06 us
  transfers between devices with their start and end apart: 2 -> 2, of which waited for: 0 -> 1; matrix products, arithmetic and copies ran while one was open for 1% -> 0% of each run, Pallas kernels for 9% -> 6%
where the time goes in v1:
time: 67.3 us; the launch traced here: 66.3 us
  blocking collectives  52.9 us (79%)
  Pallas kernels  9.4 us (14%)
  local copies, waits for them, and re-layouts  2.06 us (3%)
  between operations  0.69 us (1%)
    all_to_all x1, blocking collectives, rest(): got = lax.all_to_all(sent, 'narrow', 0, 0)  32.6 us
    all_to_all x1, blocking collectives, rest(): lax.all_to_all(slots, 'wide', 0, 0, axis_index_groups=same_core)  20.3 us
    pallas_call x1, Pallas kernels, first(): pl.pallas_call(first_kernel, out_shape=(jax.ShapeDtypeStruct((128,), jnp....  4.12 us
    pallas_call x1, Pallas kernels, product(): pl.pallas_call(functools.partial(product_kernel, form), out_shape=jax.Sha...  3.13 us
    unnamed x6, local copies, waits for them, and re-layouts  2.06 us
    pallas_call x1, Pallas kernels, spread(): pl.pallas_call(functools.partial(spread_kernel, form, q), out_shape=jax.S...  1.48 us
  transfers between devices with their start and end apart: 2, of which 1 were waited for; matrix products, arithmetic and copies ran while one was open for 0% of the time, Pallas kernels for 6%

profile of v1, /device:TPU:2, one launch (start us, length us, event | category | flops | bytes accessed | tf_op | source)
XLA Modules:
  0.0 66.3 jit_solution(13233151330010943838)
XLA Ops:
  0.0 0.0 collective-permute-start.1
  0.0 0.0 copy-start
  0.0 0.7 %copy-done = s32[640]{0:T(1024)S(1)} copy-done((s32[640]{0:T(1024)S(1)}, s32[640]{0:T(1024)}, u32[]{:S(2)}) %copy-start) | copy-done | bytes 2584
  0.7 0.0 copy-start.1
  0.7 0.7 copy-done.1
  1.3 4.1 %first.1 = (s32[128]{0:T(128)S(1)}, s32[1]{0:T(128)}, f32[160,256]{1,0:T(8,128)S(1)}, f32[160,256]{1,0:T(8,128)S(1)}) custom-call(s32[64]{0:T(128)} %occ.1, s32[5,128]{1,0:T(8,128)S(1)} %bitcast.6, s32[4]{0:T(128)S(1)} %copy-done.1, f32[160,4,640]{2,1,0:T(4,128)} %bitcast.11), custom_call_target="tpu_custom_call" | custom-call | tf_op jit(solution)/shard_map/first/pallas_call | solution.py:133
  5.5 0.6 collective-permute-start.2
  6.7 0.0 collective-permute-done.1
  6.7 0.4 collective-permute-done.2
  7.1 58.5 %conditional.1 = (f32[4,4,40,40]{3,2,1,0:T(8,128)S(1)}) conditional(s32[]{:T(128)} %bitcast.2, (s32[128]{0:T(128)S(1)}, s32[64]{0:T(128)}, f32[160,4,640]{2,1,0:T(4,128)}, f32[4,160,640]{2,1,0:T(8,128)}, f32[4,160,640]{2,1,0:T(8,128)S(1)}) %tuple.25, (s32[128]{0:T(128)S(1)}, s32[64]{0:T(128)}, f32[4,160,640]{2,1,0:T(8,128)}, ...), branch_computations={%region_0.0_spmd, %region_1.0_spmd, %region_2.0_spmd} | conditional | bytes 19988556 | solution.py:337
  7.1 3.1 %product.5 = f32[16,240,128]{2,1,0:T(8,128)S(1)} custom-call(s32[128]{0:T(128)S(1)} %get-tuple-element.56.table, s32[64]{0:T(128)} %get-tuple-element.57.occ, f32[4,160,640]{2,1,0:T(8,128)} %get-tuple-element.58.a_own, f32[4,160,640]{2,1,0:T(8,128)S(1)} %get-tuple-element.59.a_other, f32[160,256]{1,0:T(8,128)S(1)} %get-tuple-element.60.w_own, ...), custom_call_target="tpu_custom_call" | custom-call | tf_op jit(solution)/shard_map/cond/branch_2_fun/product/pallas_call | solution.py:200
  10.2 32.6 %all_to_all.28.got = f32[16,240,128]{2,1,0:T(8,128)S(1)} all-to-all(f32[16,240,128]{2,1,0:T(8,128)S(1)} %product.5), channel_id=1, replica_groups=mesh['wide'=16,'narrow'=16] {'narrow'}, dimensions={0} | all-to-all | bytes 3932160 | tf_op jit(solution)/shard_map/cond/branch_2_fun/all_to_all | solution.py:316
  42.8 1.5 %spread.5 = f32[8,40,256]{2,1,0:T(8,128)S(1)} custom-call(s32[128]{0:T(128)S(1)} %get-tuple-element.56.table, f32[16,240,128]{2,1,0:T(8,128)S(1)} %all_to_all.28.got), custom_call_target="tpu_custom_call" | custom-call | tf_op jit(solution)/shard_map/cond/branch_2_fun/spread/pallas_call | solution.py:272
  44.3 20.3 %all_to_all.29.got = f32[8,40,256]{2,1,0:T(8,128)S(1)} all-to-all(f32[8,40,256]{2,1,0:T(8,128)S(1)} %spread.5), channel_id=1, replica_groups={{0,32,64,96,128,160,192,224},{16,48,80,112,144,176,208,240},{1,33,65,97..., dimensions={0} | all-to-all | bytes 655360 | tf_op jit(solution)/shard_map/cond/branch_2_fun/all_to_all | solution.py:319
  64.7 0.7 %finish.5 = f32[4,4,40,40]{3,2,1,0:T(8,128)S(1)} custom-call(s32[128]{0:T(128)S(1)} %get-tuple-element.56.table, f32[8,40,256]{2,1,0:T(8,128)S(1)} %all_to_all.29.got), custom_call_target="tpu_custom_call" | custom-call | tf_op jit(solution)/shard_map/cond/branch_2_fun/finish/pallas_call | solution.py:303
  65.6 0.0 copy-start.3
  65.6 0.7 %copy-done.3 = f32[4,4,40,40]{3,2,1,0:T(8,128)} copy-done((f32[4,4,40,40]{3,2,1,0:T(8,128)}, f32[4,4,40,40]{3,2,1,0:T(8,128)S(1)}, u32[]{:S(2)}) %copy-start.3) | copy-done | bytes 102424
Async XLA Ops:
  0.0 6.7 %collective-permute-start.1 = (f32[4,160,640]{2,1,0:T(8,128)}, f32[4,160,640]{2,1,0:T(8,128)S(1)}, u32[]{:S(2)}, u32[]{:S(2)}) collective-permute-start(f32[4,160,640]{2,1,0:T(8,128)} %bitcast.7), channel_id=1, source_target_pairs={{0,16},{16,0},{32,48},{48,32},{64,80},{80,64},{96,112},{112,96},{1... | collective-permute-start | bytes 4915208 | tf_op jit(solution)/shard_map/ppermute | solution.py:157
  0.0 0.7 %copy-start = (s32[640]{0:T(1024)S(1)}, s32[640]{0:T(1024)}, u32[]{:S(2)}) copy-start(s32[640]{0:T(1024)} %param.11) | copy-start | bytes 7684
  0.7 0.7 copy-start.1
  5.5 1.6 %collective-permute-start.2 = (f32[160,256]{1,0:T(8,128)S(1)}, f32[160,256]{1,0:T(8,128)S(1)}, u32[]{:S(2)}, u32[]{:S(2)}) collective-permute-start(f32[160,256]{1,0:T(8,128)S(1)} %get-tuple-element.69), channel_id=1, source_target_pairs={{0,16},{16,0},{32,48},{48,32},{64,80},{80,64},{96,112},{112,96},{1... | collective-permute-start | bytes 491528 | tf_op jit(solution)/shard_map/ppermute | solution.py:157
  65.6 0.7 %copy-start.3 = (f32[4,4,40,40]{3,2,1,0:T(8,128)}, f32[4,4,40,40]{3,2,1,0:T(8,128)S(1)}, u32[]{:S(2)}) copy-start(f32[4,4,40,40]{3,2,1,0:T(8,128)S(1)} %get-tuple-element.80) | copy-start | bytes 307204
